TPU v7x, 32 devices: a whole 2x2x4 slice. The times are simulated.
32 devices in a mesh: dp: 16 (over z, y, core), proto: 2 (over x).
Axes of the slice: x: 2, y: 2, z: 4, core: 2. Of those that a mesh axis runs over, the one named last changes fastest.
Arguments:
- feature_matrix: bfloat16 [4096, 128], P('dp'), may hold values from -64 to 64
- tangent_embed: bfloat16 [4096, 128], P('dp'), may hold values from -2 to 2
- anchor_matrix: bfloat16 [65536, 128], P('proto'), may hold values from -4 to 4
- anchor_perturbation: bfloat16 [65536, 128], P('proto'), may hold values from -0.5 to 0.5
- codes: bfloat16 [4096, 65536], P('dp', 'proto'), may hold values from 0 to 3, as said below
- partner_lookup: int32 [4096], P('dp'), may hold values from 0 to 4095, as said below
Outputs:
- hvp_embed: bfloat16 [4096, 128], P('dp')
- hvp_proto: bfloat16 [65536, 128], P('proto')
Inputs may be any that keep to these rules, and one draw needn't show every extreme that they name: partner_lookup[partner_lookup[i]] = i and partner_lookup[i] != i for every crop i. `codes`: positive.
All inputs are finite; a program needn't handle non-finite values.
Results may differ from a plain program's by a relative error of at most 0.0051.
Values may be sent and summed in bfloat16 or wider, within the bound.
A program may use at most 192 MiB of HBM per device.

v0:
```python
import jax
import jax.numpy as jnp
from jax import lax
from jax.sharding import PartitionSpec as P

softening_constant = 0.1


def aggregated_elements(left, right):
    return lax.dot_general(
        left, right, (((1,), (1,)), ((), ())), preferred_element_type=jnp.float32
    )


def reduce_along_samples(left, right):
    return lax.dot_general(
        left, right, (((0,), (0,)), ((), ())), preferred_element_type=jnp.float32
    )


def body(feature_matrix, tangent_embed, anchor_matrix, anchor_perturbation, codes, partner_lookup):
    collected_features, gathered_tan = (
        lax.all_gather(feature_matrix, "dp", axis=0, tiled=True),
        lax.all_gather(tangent_embed, "dp", axis=0, tiled=True),
    )
    traded_contributions = jnp.take(collected_features, partner_lookup, axis=0)
    swapped_tan = jnp.take(gathered_tan, partner_lookup, axis=0)
    unscaled_affinity = (
        aggregated_elements(traded_contributions, anchor_matrix) / softening_constant
    )
    similarity_direction = (
        aggregated_elements(swapped_tan, anchor_matrix)
        + aggregated_elements(traded_contributions, anchor_perturbation)
    ) / softening_constant
    local_max = jnp.max(unscaled_affinity, axis=1)
    local_mass = jnp.sum(codes, axis=1, dtype=jnp.float32)
    row_max = lax.pmax(local_max, "proto")
    exponent = jnp.exp(unscaled_affinity - row_max[:, None])
    softmax_total, weighted, line_sum_norm = lax.psum(
        (jnp.sum(exponent, axis=1), jnp.sum(exponent * similarity_direction, axis=1), local_mass),
        "proto",
    )
    model_likelihood = exponent / softmax_total[:, None]
    mean_code_vector = weighted / softmax_total
    outer_patch_multiplier = (
        softening_constant
        * line_sum_norm[:, None]
        * model_likelihood
        * (similarity_direction - mean_code_vector[:, None])
    ).astype(jnp.bfloat16)
    right_crop_factor = (
        softening_constant * (line_sum_norm[:, None] * model_likelihood - codes.astype(jnp.float32))
    ).astype(jnp.bfloat16)
    partial_embed = jnp.dot(
        outer_patch_multiplier, anchor_matrix, preferred_element_type=jnp.float32
    ) + jnp.dot(right_crop_factor, anchor_perturbation, preferred_element_type=jnp.float32)
    proto_block = lax.psum_scatter(
        reduce_along_samples(outer_patch_multiplier, traded_contributions)
        + reduce_along_samples(right_crop_factor, swapped_tan),
        "dp",
        scatter_dimension=0,
        tiled=True,
    ).astype(jnp.bfloat16)
    hvp_proto = lax.all_gather(proto_block, "dp", axis=0, tiled=True)
    summed = lax.psum(partial_embed, "proto").astype(jnp.bfloat16)
    gathered_out = lax.all_gather(summed, "dp", axis=0, tiled=True)
    hvp_embed = jnp.take(gathered_out, partner_lookup, axis=0)
    return (hvp_embed, hvp_proto)


def solution(mesh):
    in_specs = (
        P("dp", None),
        P("dp", None),
        P("proto", None),
        P("proto", None),
        P("dp", "proto"),
        P("dp"),
    )
    out_specs = (P("dp", None), P("proto", None))
    return jax.shard_map(body, mesh=mesh, in_specs=in_specs, out_specs=out_specs, check_vma=False)
```

profile of v0, /device:TPU:0, one launch (start us, length us, event | category | flops | bytes accessed | tf_op | source)
XLA Modules:
  0.0 527.9 jit_solution(4280659211437309938)
XLA Ops:
  8.7 6.9 %convert_reduce_fusion = f32[256]{0:T(256)S(1)} fusion(bf16[256,32768]{1,0:T(8,128)(2,1)} %param.12), kind=kLoop, calls=%fused_computation.7 | loop fusion | flops 16776960 | bytes 16778240 | tf_op jit(solution)/shard_map/reduce_sum | solution.py:36
  15.6 35.2 %all-gather.7.cloned.1.call-done = bf16[4096,128]{1,0:T(8,128)(2,1)} async-done(((bf16[256,128]{1,0:T(8,128)(2,1)}), bf16[4096,128]{1,0:T(8,128)(2,1)}) %all-gather.7.cloned.1.call-update) | async-done | bytes 1048592 | tf_op jit(solution)/shard_map/all_gather | solution.py:24
  50.8 2.1 gather_fusion.1
  52.9 16.5 %fusion.5 = f32[256,32768]{1,0:T(8,128)} fusion(bf16[32768,128]{1,0:T(8,128)(2,1)} %param.10, bf16[256,128]{1,0:T(8,128)(2,1)S(1)} %gather_fusion.1, pred[256]{0:T(512)(128)(4,1)S(1)} %compare_and_fusion), kind=kOutput, calls=%fused_computation.20 | convolution fusion | flops 2147516416 | bytes 42008832 | tf_op jit(solution)/shard_map/dot_general | solution.py:10
  69.5 20.4 %all-gather.5.cloned.1.call-done = bf16[4096,128]{1,0:T(8,128)(2,1)} async-done(((bf16[256,128]{1,0:T(8,128)(2,1)}), bf16[4096,128]{1,0:T(8,128)(2,1)}) %all-gather.5.cloned.1.call-update) | async-done | bytes 1048592 | tf_op jit(solution)/shard_map/all_gather | solution.py:23
  89.9 2.1 gather_fusion
  92.0 16.5 %fusion.9 = (f32[256]{0:T(256)S(1)}, f32[256,32768]{1,0:T(8,128)}) fusion(bf16[32768,128]{1,0:T(8,128)(2,1)} %param.10, bf16[256,128]{1,0:T(8,128)(2,1)S(1)} %gather_fusion, pred[256]{0:T(512)(128)(4,1)S(1)} %compare_and_fusion), kind=kOutput, calls=%fused_computation.28 | convolution fusion | flops 2164293376 | bytes 42009856 | tf_op jit(solution)/shard_map/dot_general | solution.py:10
  108.5 4.9 pmax.7
  113.4 37.7 %fusion.4 = (f32[256]{0:T(256)S(1)}, f32[256]{0:T(256)S(1)}, f32[256,32768]{1,0:T(8,128)}) fusion(f32[256,32768]{1,0:T(8,128)} %get-tuple-element.11, f32[256]{0:T(256)S(1)} %pmax.7, f32[256,32768]{1,0:T(8,128)} %fusion.5, bf16[32768,128]{1,0:T(8,128)(2,1)} %param.11, bf16[256,128]{1,0:T(8,128)(2,1)S(1)} %gather_fusion, pred[256]{0:T(512)(128)(4,1)S(1)} %compare_and_fusion), kind=kOutput, calls=%fused_computation.15 | convolution fusion | flops 2197847552 | bytes 109120768 | tf_op jit(solution)/shard_map/dot_general | solution.py:10
  151.1 5.1 all-reduce
  156.2 32.7 %fusion.2 = (bf16[256,32768]{1,0:T(8,128)(2,1)}, bf16[256,32768]{1,0:T(8,128)(2,1)S(1)}) fusion(bf16[256,32768]{1,0:T(8,128)(2,1)} %param.12, f32[256]{0:T(256)S(1)} %get-tuple-element.7, f32[256]{0:T(256)S(1)} %get-tuple-element.6, f32[256,32768]{1,0:T(8,128)} %get-tuple-element.11, f32[256]{0:T(256)S(1)} %pmax.7, f32[256,32768]{1,0:T(8,128)} %get-tuple-element.12, ...), kind=kLoop, calls=%fused_computation.10 | loop fusion | flops 92274688 | bytes 117445632 | tf_op jit(solution)/shard_map/convert_element_type | solution.py:53
  188.9 8.8 %fusion.8 = f32[32768,128]{1,0:T(8,128)} fusion(bf16[256,32768]{1,0:T(8,128)(2,1)S(1)} %get-tuple-element.9, bf16[256,128]{1,0:T(8,128)(2,1)S(1)} %gather_fusion, pred[256]{0:T(512)(128)(4,1)S(1)} %compare_and_fusion), kind=kOutput, calls=%fused_computation.27 | convolution fusion | flops 2147516416 | bytes 33620224 | tf_op jit(solution)/shard_map/dot_general | solution.py:16
  197.7 2.0 copy-done
  199.7 20.9 %convolution_add_fusion.1 = f32[32768,128]{1,0:T(8,128)} fusion(f32[32768,128]{1,0:T(8,128)} %fusion.8, bf16[256,32768]{1,0:T(8,128)(2,1)} %get-tuple-element.8, bf16[256,128]{1,0:T(8,128)(2,1)S(1)} %gather_fusion.1, pred[256]{0:T(512)(128)(4,1)S(1)} %compare_and_fusion), kind=kOutput, calls=%fused_computation.8 | convolution fusion | flops 2151710720 | bytes 50397440 | tf_op jit(solution)/shard_map/dot_general | solution.py:16
  220.9 12.8 %fusion.10 = f32[256,128]{1,0:T(8,128)S(1)} fusion(bf16[256,32768]{1,0:T(8,128)(2,1)} %copy-done, bf16[32768,128]{1,0:T(8,128)(2,1)} %param.10), kind=kOutput, calls=%fused_computation.29 | convolution fusion | flops 2147483648 | bytes 25296896 | tf_op jit(solution)/shard_map/dot_general | solution.py:54
  233.7 15.0 %convolution_add_fusion.2 = f32[256,128]{1,0:T(8,128)S(1)} fusion(f32[256,128]{1,0:T(8,128)S(1)} %fusion.10, bf16[256,32768]{1,0:T(8,128)(2,1)} %get-tuple-element.8, bf16[32768,128]{1,0:T(8,128)(2,1)} %param.11), kind=kOutput, calls=%fused_computation.16 | convolution fusion | flops 2147516416 | bytes 25427968 | tf_op jit(solution)/shard_map/dot_general | solution.py:56
  248.8 10.0 %all-reduce.2 = bf16[256,128]{1,0:T(8,128)(2,1)} all-reduce(f32[256,128]{1,0:T(8,128)S(1)} %convolution_add_fusion.2), channel_id=1, replica_groups=mesh['dp'=16,'proto'=2] {'proto'}, use_global_device_ids=true, to_apply=%region_8.10 | all-reduce | flops 32768 | bytes 196608 | tf_op jit(solution)/shard_map/psum | solution.py:65
  258.9 139.4 %reduce-scatter.2.cloned.1.call-done = f32[2048,128]{1,0:T(8,128)} async-done(((f32[32768,128]{1,0:T(8,128)}), f32[2048,128]{1,0:T(8,128)}) %reduce-scatter.2.cloned.1.call-update) | async-done | bytes 1048592 | tf_op jit(solution)/shard_map/reduce_scatter | solution.py:57
  398.2 2.1 convert_element_type.20
  400.3 37.5 %all-gather.9.cloned.1.call-done = bf16[4096,128]{1,0:T(8,128)(2,1)} async-done(((bf16[256,128]{1,0:T(8,128)(2,1)}), bf16[4096,128]{1,0:T(8,128)(2,1)}) %all-gather.9.cloned.1.call-update) | async-done | bytes 1048592 | tf_op jit(solution)/shard_map/all_gather | solution.py:66
  437.8 2.1 gather_fusion.2
  439.9 0.7 broadcast_select_fusion.2
  440.6 73.6 %all-gather.11.cloned.1.call-done = bf16[32768,128]{1,0:T(8,128)(2,1)} async-done(((bf16[2048,128]{1,0:T(8,128)(2,1)}), bf16[32768,128]{1,0:T(8,128)(2,1)}) %all-gather.11.cloned.1.call-update) | async-done | bytes 8388624 | tf_op jit(solution)/shard_map/all_gather | solution.py:64
  514.2 7.1 %copy.11 = bf16[32768,128]{1,0:T(8,128)(2,1)} copy(bf16[32768,128]{1,0:T(8,128)(2,1)} %all-gather.11.cloned.1.call-done) | data formatting | bytes 16777216
  (18 shorter events, 1.9 us)
Async XLA Ops:
  7.2 8.4 %copy-start.1 = (s32[256]{0:T(256)S(1)}, s32[256]{0:T(256)}, u32[]{:S(2)}) copy-start(s32[256]{0:T(256)} %param.13) | copy-start | bytes 3076
  7.2 43.7 %all-gather.7.cloned.1.call-start = ((), (), s32[]{:S(2)}) async-start(), calls=%async_computation.2 | async-start | bytes 1114112 | tf_op jit(solution)/shard_map/all_gather | solution.py:24
  7.9 82.0 %all-gather.5.cloned.1.call-start = ((), (), s32[]{:S(2)}) async-start(), calls=%async_computation.1 | async-start | bytes 1114112 | tf_op jit(solution)/shard_map/all_gather | solution.py:23
  8.7 389.6 %reduce-scatter.2.cloned.1.call-start = ((), (), s32[]{:S(2)}) async-start(), calls=%async_computation.4 | async-start | bytes 17825792 | tf_op jit(solution)/shard_map/reduce_scatter | solution.py:57
  188.9 10.8 %copy-start = (bf16[256,32768]{1,0:T(8,128)(2,1)}, bf16[256,32768]{1,0:T(8,128)(2,1)S(1)}, u32[]{:S(2)}) copy-start(bf16[256,32768]{1,0:T(8,128)(2,1)S(1)} %get-tuple-element.9) | copy-start | bytes 50331652
  220.6 217.2 %all-gather.9.cloned.1.call-start = ((), (), s32[]{:S(2)}) async-start(), calls=%async_computation.3 | async-start | bytes 1114112 | tf_op jit(solution)/shard_map/all_gather | solution.py:66
  258.8 255.4 %all-gather.11.cloned.1.call-start = ((), (), s32[]{:S(2)}) async-start(), calls=%async_computation.5 | async-start | bytes 8912896 | tf_op jit(solution)/shard_map/all_gather | solution.py:64
Sparse Core Ops, SparseCore 0:
  10.2 40.6 all-gather.6
  53.0 36.8 all-gather.4
  220.8 177.4 reduce-scatter.1
  400.8 36.9 all-gather.8
  440.4 73.7 all-gather.10
where the time goes:
time: 528 us
  waiting for transfers between devices  308 us (58%)
  matrix products  128 us (24%)
  other arithmetic  42.4 us (8%)
  blocking collectives  20 us (4%)
  local copies, waits for them, and re-layouts  15.3 us (3%)
  between operations  13.8 us (3%)
    reduce_scatter x1, waiting for transfers between devices, body(): lax.psum_scatter(reduce_along_samples(outer_patch_multiplier, traded_cont...  139 us
    all_gather x1, waiting for transfers between devices, body(): hvp_proto = lax.all_gather(proto_block, 'dp', axis=0, tiled=True)  73.6 us
    dot_general x3, matrix products, aggregated_elements(): lax.dot_general(left, right, (((1,), (1,)), ((), ())), preferred_element_...  70.7 us
    all_gather x1, waiting for transfers between devices, body(): gathered_out = lax.all_gather(summed, 'dp', axis=0, tiled=True)  37.5 us
    all_gather x1, waiting for transfers between devices, body(): lax.all_gather(tangent_embed, 'dp', axis=0, tiled=True)  35.2 us
    convert_element_type x1, other arithmetic, body(): right_crop_factor = (softening_constant * (line_sum_norm[:, None] * model...  32.7 us
    dot_general x2, matrix products, reduce_along_samples(): lax.dot_general(left, right, (((0,), (0,)), ((), ())), preferred_element_...  29.7 us
    all_gather x1, waiting for transfers between devices, body(): lax.all_gather(feature_matrix, 'dp', axis=0, tiled=True)  20.4 us
  transfers between devices with their start and end apart: 5, of which 5 were waited for; matrix products, arithmetic and copies ran while one was open for 11% of the time, Pallas kernels for 0%

commit v1 on v0

v1 whole, which is shorter than its diff:
```python
import functools
import math

import jax
import jax.numpy as jnp
from jax import lax
from jax.experimental import pallas as pl
from jax.experimental.pallas import tpu as pltpu
from jax.sharding import PartitionSpec as P

MESH = pl.DeviceIdType.MESH
F32 = jnp.float32
BF16 = jnp.bfloat16
LOG2E = math.log2(math.e)
TEMP = 0.1
SCALE = LOG2E / TEMP
LANES = 128
MIB = 1024 * 1024


def place(n):
    d = lax.axis_index("dp")
    return d // 4, (d // 2) % 2, d % 2, n // 4


def index_of(a, b, c):
    return (a * 2 + b) * 2 + c


def greet(a, b, c, length):
    barrier = pltpu.get_barrier_semaphore()

    def hello(target):
        pl.semaphore_signal(barrier, inc=1, device_id={"dp": target}, device_id_type=MESH)

    hello(index_of(a, b, 1 - c))
    hello(index_of(a, 1 - b, c))

    @pl.when(a > 0)
    def _():
        hello(index_of(a - 1, b, c))

    @pl.when(a < length - 1)
    def _():
        hello(index_of(a + 1, b, c))

    peers = 2 + jnp.where(a > 0, 1, 0) + jnp.where(a < length - 1, 1, 0)
    pl.semaphore_wait(barrier, peers)


class Copies:
    def __init__(self, arrays, block, kind, target):
        self.copies = [
            pltpu.make_async_remote_copy(
                src_ref=out.at[block],
                dst_ref=out.at[block],
                send_sem=send.at[kind, block],
                recv_sem=recv.at[block],
                device_id={"dp": target},
                device_id_type=MESH,
            )
            for out, send, recv in arrays
        ]

    def start(self):
        for copy in self.copies:
            copy.start()

    def wait_send(self):
        for copy in self.copies:
            copy.wait_send()

    def wait_recv(self):
        for copy in self.copies:
            copy.wait_recv()


def gather_steps(arrays, a, b, c, length):
    def copy(block, kind, target):
        return Copies(arrays, block, kind, target)

    right, left = index_of(a + 1, b, c), index_of(a - 1, b, c)
    pair, twin = index_of(a, 1 - b, c), index_of(a, b, 1 - c)

    def line_block(pos):
        return index_of(pos, b, c)

    def spread(block, to_right, to_left):
        if to_right:

            @pl.when(a < length - 1)
            def _():
                copy(block, 0, right).start()

        if to_left:

            @pl.when(a > 0)
            def _():
                copy(block, 1, left).start()

        copy(block, 2, pair).start()
        copy(block, 3, twin).start()

    def from_pair(pos):
        block = index_of(pos, 1 - b, c)
        copy(block, 2, pair).wait_recv()
        copy(block, 3, twin).start()

    spread(line_block(a), True, True)
    for k in range(1, length):

        @pl.when(a - k >= 0)
        def _():
            copy(line_block(a - k), 0, right).wait_recv()
            spread(line_block(a - k), True, False)

        @pl.when(a + k < length)
        def _():
            copy(line_block(a + k), 1, left).wait_recv()
            spread(line_block(a + k), False, True)

    from_pair(a)
    for k in range(1, length):

        @pl.when(a - k >= 0)
        def _():
            from_pair(a - k)

        @pl.when(a + k < length)
        def _():
            from_pair(a + k)

    for pos in range(length):
        for side in range(2):
            copy(index_of(pos, side, 1 - c), 3, twin).wait_recv()
    for pos in range(length):
        copy(line_block(pos), 2, pair).wait_send()
        for side in range(2):
            copy(index_of(pos, side, c), 3, twin).wait_send()

        @pl.when(jnp.logical_and(a < length - 1, pos <= a))
        def _():
            copy(line_block(pos), 0, right).wait_send()

        @pl.when(jnp.logical_and(a > 0, pos >= a))
        def _():
            copy(line_block(pos), 1, left).wait_send()


def gather_kernel(n, x, out, send, recv, local):
    a, b, c, length = place(n)
    own = pltpu.make_async_copy(x, out.at[index_of(a, b, c)], local)
    own.start()
    greet(a, b, c, length)
    own.wait()
    gather_steps([(out, send, recv)], a, b, c, length)


def gather_call(n, x, collective_id):
    return pl.pallas_call(
        functools.partial(gather_kernel, n),
        out_shape=jax.ShapeDtypeStruct((n,) + x.shape, x.dtype),
        in_specs=[pl.BlockSpec(memory_space=pltpu.VMEM)],
        out_specs=pl.BlockSpec(memory_space=pltpu.VMEM),
        scratch_shapes=[
            pltpu.SemaphoreType.DMA((4, n)),
            pltpu.SemaphoreType.DMA((n,)),
            pltpu.SemaphoreType.DMA,
        ],
        compiler_params=pltpu.CompilerParams(
            collective_id=collective_id, has_side_effects=True, vmem_limit_bytes=32 * MIB
        ),
    )(x)


def reduce_kernel(n, parts, embed, out, embeds, own1, recv1, recv2, recv_l, recv_r, out2, out_l, out_r,
                  load, s1, r1, s2, r2, sl, sr, rl, rr, local, g_send, g_recv, e_send, e_recv):
    a, b, c, length = place(n)
    rows = parts.shape[1]
    step = 256
    right, left = index_of(a + 1, b, c), index_of(a - 1, b, c)
    pair, twin = index_of(a, 1 - b, c), index_of(a, b, 1 - c)
    embed_in = pltpu.make_async_copy(embed, embeds.at[index_of(a, b, c)], local.at[0])
    embed_in.start()

    def order(j):
        return jnp.where(a < length // 2, (a - 1 - j + 2 * length) % length, (a + 1 + j) % length)

    def remote(src, dst, send, recv, target):
        return pltpu.make_async_remote_copy(
            src_ref=src, dst_ref=dst, send_sem=send, recv_sem=recv, device_id={"dp": target}, device_id_type=MESH
        )

    def to_twin(pos, side):
        k = pos * 2 + side
        return remote(parts.at[index_of(pos, side, 1 - c)], recv1.at[k], s1.at[k], r1.at[k], twin)

    def load_own(pos, side):
        k = pos * 2 + side
        return pltpu.make_async_copy(parts.at[index_of(pos, side, c)], own1.at[k], load.at[k])

    def to_pair(pos):
        return remote(out2.at[pos], recv2.at[pos], s2.at[pos], r2.at[pos], pair)

    def to_right(pos):
        return remote(out_r.at[pos], recv_l.at[pos], sr.at[pos], rl.at[pos], right)

    def to_left(pos):
        return remote(out_l.at[pos], recv_r.at[pos], sl.at[pos], rr.at[pos], left)

    for j in range(length):
        for side in (1 - b, b):
            load_own(order(j), side).start()
    greet(a, b, c, length)
    for side in (1 - b, b):
        for j in range(length):
            to_twin(order(j), side).start()
    embed_in.wait()

    def added(dst, srcs):
        def one(i, carry):
            at = pl.ds(pl.multiple_of(i * step, step), step)
            total = srcs[0][at, :].astype(F32)
            for src in srcs[1:]:
                total = total + src[at, :].astype(F32)
            dst[at, :] = total.astype(dst.dtype)
            return carry

        lax.fori_loop(0, rows // step, one, 0)

    for j in range(length):
        pos = order(j)
        k = pos * 2 + 1 - b
        load_own(pos, 1 - b).wait()
        to_twin(pos, 1 - b).wait_recv()
        added(out2.at[pos], [own1.at[k], recv1.at[k]])
        to_pair(pos).start()

    for j in range(length):
        load_own(order(j), b).wait()
        to_twin(order(j), b).wait_recv()

    def terms(pos):
        k = pos * 2 + b
        return [own1.at[k], recv1.at[k], recv2.at[pos]]

    for t in range(length - 1):
        r_pos = length - 1 - (t - a)
        l_pos = t - (length - 1 - a)

        @pl.when(jnp.logical_and(t - a >= 0, r_pos > a))
        def _():
            to_pair(r_pos).wait_recv()

            @pl.when(a > 0)
            def _():
                to_right(r_pos).wait_recv()
                added(out_r.at[r_pos], terms(r_pos) + [recv_l.at[r_pos]])

            @pl.when(a == 0)
            def _():
                added(out_r.at[r_pos], terms(r_pos))

            to_right(r_pos).start()

        @pl.when(jnp.logical_and(l_pos >= 0, l_pos < a))
        def _():
            to_pair(l_pos).wait_recv()

            @pl.when(a < length - 1)
            def _():
                to_left(l_pos).wait_recv()
                added(out_l.at[l_pos], terms(l_pos) + [recv_r.at[l_pos]])

            @pl.when(a == length - 1)
            def _():
                added(out_l.at[l_pos], terms(l_pos))

            to_left(l_pos).start()

    to_pair(a).wait_recv()
    final = own1.at[a * 2 + b]

    @pl.when(a > 0)
    def _():
        to_right(a).wait_recv()

    @pl.when(a < length - 1)
    def _():
        to_left(a).wait_recv()

    @pl.when(a == 0)
    def _():
        added(final, terms(a) + [recv_r.at[a]])

    @pl.when(a == length - 1)
    def _():
        added(final, terms(a) + [recv_l.at[a]])

    @pl.when(jnp.logical_and(a > 0, a < length - 1))
    def _():
        added(final, terms(a) + [recv_l.at[a], recv_r.at[a]])

    done = pltpu.make_async_copy(final, out.at[index_of(a, b, c)], local.at[1])
    done.start()
    done.wait()
    gather_steps([(embeds, e_send, e_recv), (out, g_send, g_recv)], a, b, c, length)

    for pos in range(length):
        for side in range(2):
            to_twin(pos, side).wait_send()
        to_pair(pos).wait_send()

        @pl.when(pos > a)
        def _():
            to_right(pos).wait_send()

        @pl.when(pos < a)
        def _():
            to_left(pos).wait_send()


def reduce_call(n, parts, embed, collective_id):
    length = n // 4
    rows, width = parts.shape[1:]
    sems = pltpu.SemaphoreType.DMA
    block = lambda count: pltpu.VMEM((count, rows, width), BF16)
    return pl.pallas_call(
        functools.partial(reduce_kernel, n),
        out_shape=(
            jax.ShapeDtypeStruct(parts.shape, BF16),
            jax.ShapeDtypeStruct((n,) + embed.shape, BF16),
        ),
        in_specs=[pl.BlockSpec(memory_space=pl.ANY)] * 2,
        out_specs=[pl.BlockSpec(memory_space=pl.ANY)] * 2,
        scratch_shapes=[
            block(2 * length), block(2 * length), block(length), block(length), block(length),
            block(length), block(length), block(length),
            sems((2 * length,)), sems((2 * length,)), sems((2 * length,)), sems((length,)), sems((length,)),
            sems((length,)), sems((length,)), sems((length,)), sems((length,)), sems((2,)),
            sems((4, n)), sems((n,)), sems((4, n)), sems((n,)),
        ],
        compiler_params=pltpu.CompilerParams(
            collective_id=collective_id, has_side_effects=True, vmem_limit_bytes=48 * MIB
        ),
    )(parts, embed)


def dot_t(left, right):
    return lax.dot_general(left, right, (((1,), (1,)), ((), ())), preferred_element_type=F32)


def stats_kernel(rows_ref, tans_ref, a_ref, b_ref, codes_ref, out_ref, top, total, weighted, mass):
    i = pl.program_id(0)
    chunk = a_ref.shape[0]

    @pl.when(i == 0)
    def _():
        top[...] = jnp.full_like(top, -1e30)
        total[...] = jnp.zeros_like(total)
        weighted[...] = jnp.zeros_like(weighted)
        mass[...] = jnp.zeros_like(mass)

    s = dot_t(rows_ref[...], a_ref[...])
    pairs = jnp.concatenate([a_ref[...], b_ref[...]], axis=1)
    tan = dot_t(jnp.concatenate([tans_ref[...], rows_ref[...]], axis=1), pairs)
    cols = [slice(k, k + LANES) for k in range(0, chunk, LANES)]
    old = top[...]
    new = functools.reduce(jnp.maximum, [s[:, k] for k in cols], old)
    fade = jnp.exp2((old - new) * SCALE)
    z, w, q = total[...] * fade, weighted[...] * fade, mass[...]
    for k in cols:
        e = jnp.exp2((s[:, k] - new) * SCALE)
        z = z + e
        w = w + e * tan[:, k]
        q = q + codes_ref[:, k].astype(F32)
    top[...], total[...], weighted[...], mass[...] = new, z, w, q

    @pl.when(i == pl.num_programs(0) - 1)
    def _():
        peak = jnp.max(top[...], axis=1, keepdims=True)
        scale = jnp.exp2((top[...] - peak) * SCALE)
        lane = lax.broadcasted_iota(jnp.int32, out_ref.shape, 1)
        values = [
            peak,
            jnp.sum(total[...] * scale, axis=1, keepdims=True),
            jnp.sum(weighted[...] * scale, axis=1, keepdims=True),
            jnp.sum(mass[...], axis=1, keepdims=True),
        ]
        out = jnp.zeros(out_ref.shape, F32)
        for k, v in enumerate(values):
            out = jnp.where(lane == k, v, out)
        out_ref[...] = out


def stats_call(rows, tans, anchors, moves, codes):
    crops, width = rows.shape
    protos = anchors.shape[0]
    chunk = math.gcd(protos, 1024)
    whole = pl.BlockSpec((crops, width), lambda i: (0, 0))
    block = pl.BlockSpec((chunk, width), lambda i: (i, 0))
    return pl.pallas_call(
        stats_kernel,
        grid=(protos // chunk,),
        out_shape=jax.ShapeDtypeStruct((crops, LANES), F32),
        in_specs=[whole, whole, block, block, pl.BlockSpec((crops, chunk), lambda i: (0, i))],
        out_specs=pl.BlockSpec((crops, LANES), lambda i: (0, 0)),
        scratch_shapes=[pltpu.VMEM((crops, LANES), F32)] * 4,
        compiler_params=pltpu.CompilerParams(vmem_limit_bytes=40 * MIB),
    )(rows, tans, anchors, moves, codes)


def weights_kernel(rows_ref, tans_ref, a_ref, b_ref, codes_ref, stats_ref, part_ref, embed_ref):
    i = pl.program_id(0)

    @pl.when(i == 0)
    def _():
        embed_ref[...] = jnp.zeros_like(embed_ref)

    s = dot_t(rows_ref[...], a_ref[...])
    pairs = jnp.concatenate([a_ref[...], b_ref[...]], axis=1)
    tan = dot_t(jnp.concatenate([tans_ref[...], rows_ref[...]], axis=1), pairs)
    peak, gain, mean = stats_ref[:, 0:1], stats_ref[:, 1:2], stats_ref[:, 2:3]
    p = jnp.exp2((s - peak) * SCALE) * gain
    u = (p * (tan - mean)).astype(BF16)
    v = (TEMP * (p - codes_ref[...].astype(F32))).astype(BF16)
    embed_ref[...] += jnp.dot(u, a_ref[...], preferred_element_type=F32) + jnp.dot(
        v, b_ref[...], preferred_element_type=F32
    )
    both = jnp.concatenate([u, v], axis=0)
    ends = jnp.concatenate([rows_ref[...], tans_ref[...]], axis=0)
    part_ref[...] = lax.dot_general(
        both, ends, (((0,), (0,)), ((), ())), preferred_element_type=F32
    ).astype(BF16)


def weights_call(rows, tans, anchors, moves, codes, stats):
    crops, width = rows.shape
    protos = anchors.shape[0]
    chunk = math.gcd(protos, 1024)
    whole = pl.BlockSpec((crops, width), lambda i: (0, 0))
    block = pl.BlockSpec((chunk, width), lambda i: (i, 0))
    return pl.pallas_call(
        weights_kernel,
        grid=(protos // chunk,),
        out_shape=(
            jax.ShapeDtypeStruct((protos, width), BF16),
            jax.ShapeDtypeStruct((crops, width), F32),
        ),
        in_specs=[
            whole, whole, block, block,
            pl.BlockSpec((crops, chunk), lambda i: (0, i)),
            pl.BlockSpec((crops, LANES), lambda i: (0, 0)),
        ],
        out_specs=(block, whole),
        compiler_params=pltpu.CompilerParams(vmem_limit_bytes=40 * MIB),
    )(rows, tans, anchors, moves, codes, stats)


def body(n, n_proto, features, tangents, anchors, moves, codes, partner):
    crops, width = features.shape
    gathered = gather_call(n, jnp.concatenate([features, tangents], axis=1), 1)
    swapped = jnp.take(gathered.reshape(n * crops, 2 * width), partner, axis=0)
    rows, tans = swapped[:, :width], swapped[:, width:]
    local = stats_call(rows, tans, anchors, moves, codes)[:, :4].T
    mine = jnp.arange(n_proto) == lax.axis_index("proto")
    every = lax.psum(jnp.where(mine[:, None, None], local[None], 0.0), "proto")
    peak = jnp.max(every[:, 0], axis=0)
    scale = jnp.exp2((every[:, 0] - peak) * SCALE)
    total = jnp.sum(every[:, 1] * scale, axis=0)
    mean = jnp.sum(every[:, 2] * scale, axis=0) / total
    mass = jnp.sum(every[:, 3], axis=0)
    stats = jnp.stack([peak, mass / total, mean], axis=1)
    stats = jnp.pad(stats, ((0, 0), (0, LANES - 3)))
    parts, embed = weights_call(rows, tans, anchors, moves, codes, stats)
    embed = lax.psum(embed, "proto").astype(BF16)
    protos = anchors.shape[0]
    out, embeds = reduce_call(n, parts.reshape(n, protos // n, width), embed, 2)
    hvp_embed = jnp.take(embeds.reshape(n * crops, width), partner, axis=0)
    return hvp_embed, out.reshape(protos, width)


def solution(mesh):
    in_specs = (
        P("dp", None),
        P("dp", None),
        P("proto", None),
        P("proto", None),
        P("dp", "proto"),
        P("dp"),
    )
    out_specs = (P("dp", None), P("proto", None))
    return jax.shard_map(
        functools.partial(body, mesh.shape["dp"], mesh.shape["proto"]),
        mesh=mesh,
        in_specs=in_specs,
        out_specs=out_specs,
        check_vma=False,
    )
```

time: 528 us -> 241 us (0.46)
  waiting for transfers between devices: 308 us -> 0 us
  Pallas kernels: 0 us -> 204 us
  matrix products: 128 us -> 0 us
  other arithmetic: 42.4 us -> 3.24 us
  between operations: 13.8 us -> 0.76 us
    pallas_call x0 -> x4, Pallas kernels: none -> 204 us  [the longest x1 113 us: reduce_call(): pl.pallas_call(functools.partial(reduce_kernel, n), out_shape=(jax.ShapeD...]
    all_gather x4 -> x0, waiting for transfers between devices: 167 us -> none  [the longest x1 73.6 us: body(): hvp_proto = lax.all_gather(proto_block, 'dp', axis=0, tiled=True)]
    reduce_scatter x1 -> x0, waiting for transfers between devices: 139 us -> none  [body(): lax.psum_scatter(reduce_along_samples(outer_patch_multiplier, traded_cont...]
    dot_general x7 -> x0, matrix products: 128 us -> none  [the longest x3 70.7 us: aggregated_elements(): lax.dot_general(left, right, (((1,), (1,)), ((), ())), preferred_element_...]
    convert_element_type x2 -> x0, other arithmetic: 34.8 us -> none  [the longest x1 32.7 us: body(): right_crop_factor = (softening_constant * (line_sum_norm[:, None] * model...]
    reduce_sum x1 -> x2, other arithmetic: 6.85 us -> 0.05 us  [the longest x1 0.03 us: body(): total = jnp.sum(every[:, 1] * scale, axis=0)]
  transfers between devices with their start and end apart: 5 -> 0, of which waited for: 5 -> 0; matrix products, arithmetic and copies ran while one was open for 11% -> 0% of each run, Pallas kernels for 0% -> 0%
where the time goes in v1:
time: 241 us; the launch traced here: 239 us
  Pallas kernels  204 us (85%)
  local copies, waits for them, and re-layouts  16.1 us (7%)
  blocking collectives  15.2 us (6%)
  other arithmetic  3.24 us (1%)
    pallas_call x1, Pallas kernels, reduce_call(): pl.pallas_call(functools.partial(reduce_kernel, n), out_shape=(jax.ShapeD...  113 us
    pallas_call x1, Pallas kernels, weights_call(): pl.pallas_call(weights_kernel, grid=(protos // chunk,), out_shape=(jax.Sh...  38.7 us
    pallas_call x1, Pallas kernels, stats_call(): pl.pallas_call(stats_kernel, grid=(protos // chunk,), out_shape=jax.Shape...  29.2 us
    pallas_call x1, Pallas kernels, gather_call(): pl.pallas_call(functools.partial(gather_kernel, n), out_shape=jax.ShapeDt...  22.8 us
    unnamed x5, local copies, waits for them, and re-layouts  13.9 us
    psum x1, blocking collectives, body(): embed = lax.psum(embed, 'proto').astype(BF16)  10.2 us
    psum x1, blocking collectives, body(): every = lax.psum(jnp.where(mine[:, None, None], local[None], 0.0), 'proto')  5 us

profile of v1, /device:TPU:0, one launch (start us, length us, event | category | flops | bytes accessed | tf_op | source)
XLA Modules:
  0.0 239.2 jit_solution(7538703191302737644)
XLA Ops:
  0.6 0.7 compare_and_fusion
  1.3 0.7 compare_select_fusion
  2.0 0.9 pad_maximum_fusion.x
  2.9 22.8 %shard_map.77 = bf16[16,256,256]{2,1,0:T(8,128)(2,1)S(1)} custom-call(bf16[256,256]{1,0:T(8,128)(2,1)S(1)} %pad_maximum_fusion.x), custom_call_target="tpu_custom_call" | custom-call | tf_op jit(solution)/shard_map/pallas_call | solution.py:160
  25.7 1.2 gather_fusion
  26.9 0.1 broadcast_select_fusion
  27.0 0.0 copy-start
  27.0 3.4 %copy-done = bf16[32768,128]{1,0:T(8,128)(2,1)S(1)} copy-done((bf16[32768,128]{1,0:T(8,128)(2,1)S(1)}, bf16[32768,128]{1,0:T(8,128)(2,1)}, u32[]{:S(2)}) %copy-start) | copy-done | bytes 8388632
  30.4 29.2 %shard_map.78 = f32[256,128]{1,0:T(8,128)S(1)} custom-call(bf16[256,128]{1,0:T(8,128)(2,1)S(1)} %get-tuple-element.15.rows_ref, bf16[256,128]{1,0:T(8,128)(2,1)S(1)} %get-tuple-element.14.tans_ref, bf16[32768,128]{1,0:T(8,128)(2,1)S(1)} %copy-done, bf16[32768,128]{1,0:T(8,128)(2,1)} %b_ref.3, bf16[256,32768]{1,0:T(8,128)(2,1)} %codes_ref.3), custom_call_target="tpu_custom_call" | custom-call | tf_op jit(solution)/shard_map/pallas_call | solution.py:402
  59.6 0.1 copy.21
  59.6 0.1 broadcast_select_fusion.2
  59.7 5.0 %psum.14 = f32[2,4,256]{2,0,1:T(2,128)S(1)} all-reduce(f32[2,4,256]{2,0,1:T(2,128)S(1)} %broadcast_select_fusion.2), channel_id=1, replica_groups=mesh['dp'=16,'proto'=2] {'proto'}, use_global_device_ids=true, to_apply=%region_0.1 | all-reduce | flops 2048 | bytes 16384 | tf_op jit(solution)/shard_map/psum | solution.py:467
  64.8 0.1 copy.22
  65.0 38.7 %shard_map.79 = (bf16[32768,128]{1,0:T(8,128)(2,1)S(1)}, f32[256,128]{1,0:T(8,128)S(1)}) custom-call(bf16[256,128]{1,0:T(8,128)(2,1)S(1)} %get-tuple-element.15.rows_ref, bf16[256,128]{1,0:T(8,128)(2,1)S(1)} %get-tuple-element.14.tans_ref, bf16[32768,128]{1,0:T(8,128)(2,1)} %a_ref.3, bf16[32768,128]{1,0:T(8,128)(2,1)} %b_ref.3, ...), custom_call_target="tpu_custom_call" | custom-call | tf_op jit(solution)/shard_map/pallas_call | solution.py:443
  103.7 0.0 copy-start.1
  103.7 3.4 %copy-done.1 = bf16[32768,128]{1,0:T(8,128)(2,1)} copy-done((bf16[32768,128]{1,0:T(8,128)(2,1)}, bf16[32768,128]{1,0:T(8,128)(2,1)S(1)}, u32[]{:S(2)}) %copy-start.1) | copy-done | bytes 8388632
  107.1 10.2 %all-reduce.2.embed = bf16[256,128]{1,0:T(8,128)(2,1)S(1)} all-reduce(f32[256,128]{1,0:T(8,128)S(1)} %get-tuple-element.7), channel_id=1, replica_groups=mesh['dp'=16,'proto'=2] {'proto'}, use_global_device_ids=true, to_apply=%region_5.6 | all-reduce | flops 32768 | bytes 196608 | tf_op jit(solution)/shard_map/psum | solution.py:476
  117.3 113.2 %shard_map.80 = (bf16[16,2048,128]{2,1,0:T(8,128)(2,1)}, bf16[16,256,128]{2,1,0:T(8,128)(2,1)S(1)}) custom-call(bf16[16,2048,128]{2,1,0:T(8,128)(2,1)} %bitcast.31, bf16[256,128]{1,0:T(8,128)(2,1)S(1)} %all-reduce.2.embed), custom_call_target="tpu_custom_call" | custom-call | tf_op jit(solution)/shard_map/pallas_call | solution.py:328
  230.5 0.9 gather_fusion.1
  231.4 0.7 broadcast_select_fusion.1
  232.1 7.1 %copy.26 = bf16[32768,128]{1,0:T(8,128)(2,1)} copy(bf16[32768,128]{1,0:T(8,128)(2,1)} %bitcast.34) | data formatting | bytes 16777216
  (9 shorter events, 0.1 us)
Async XLA Ops:
  27.0 3.4 %copy-start = (bf16[32768,128]{1,0:T(8,128)(2,1)S(1)}, bf16[32768,128]{1,0:T(8,128)(2,1)}, u32[]{:S(2)}) copy-start(bf16[32768,128]{1,0:T(8,128)(2,1)} %a_ref.3) | copy-start | bytes 25165828
  103.7 3.4 %copy-start.1 = (bf16[32768,128]{1,0:T(8,128)(2,1)}, bf16[32768,128]{1,0:T(8,128)(2,1)S(1)}, u32[]{:S(2)}) copy-start(bf16[32768,128]{1,0:T(8,128)(2,1)S(1)} %get-tuple-element.6) | copy-start | bytes 25165828

commit v2 on v1

--- a/solution.py
+++ b/solution.py
@@ -27,7 +27,7 @@
     return (a * 2 + b) * 2 + c
 
 
-def greet(a, b, c, length):
+def greet(a, b, c, length, n_proto=1):
     barrier = pltpu.get_barrier_semaphore()
 
     def hello(target):
@@ -44,7 +44,10 @@
     def _():
         hello(index_of(a + 1, b, c))
 
-    peers = 2 + jnp.where(a > 0, 1, 0) + jnp.where(a < length - 1, 1, 0)
+    me = lax.axis_index("proto")
+    for k in range(1, n_proto):
+        pl.semaphore_signal(barrier, inc=1, device_id={"proto": (me + k) % n_proto}, device_id_type=MESH)
+    peers = 1 + n_proto + jnp.where(a > 0, 1, 0) + jnp.where(a < length - 1, 1, 0)
     pl.semaphore_wait(barrier, peers)
 
 
@@ -168,20 +171,22 @@
             pltpu.SemaphoreType.DMA,
         ],
         compiler_params=pltpu.CompilerParams(
-            collective_id=collective_id, has_side_effects=True, vmem_limit_bytes=32 * MIB
+            collective_id=collective_id, has_side_effects=True, vmem_limit_bytes=56 * MIB
         ),
     )(x)
 
 
-def reduce_kernel(n, parts, embed, out, embeds, own1, recv1, recv2, recv_l, recv_r, out2, out_l, out_r,
-                  load, s1, r1, s2, r2, sl, sr, rl, rr, local, g_send, g_recv, e_send, e_recv):
+def reduce_kernel(n, n_proto, rows_ref, tans_ref, stats_ref, anchors, moves, codes, out, embeds,
+                  a_buf, b_buf, c_buf, parts, recv1, recv2, recv_l, recv_r, out2, out_l, out_r, embed_sum, embed_in,
+                  load, s1, r1, s2, r2, sl, sr, rl, rr, sx, rx, local, g_send, g_recv, e_send, e_recv):
     a, b, c, length = place(n)
+    me = lax.axis_index("proto")
     rows = parts.shape[1]
-    step = 256
+    step = math.gcd(rows, 256)
+    tile = math.gcd(rows, 1024)
+    tiles = rows // tile
     right, left = index_of(a + 1, b, c), index_of(a - 1, b, c)
     pair, twin = index_of(a, 1 - b, c), index_of(a, b, 1 - c)
-    embed_in = pltpu.make_async_copy(embed, embeds.at[index_of(a, b, c)], local.at[0])
-    embed_in.start()
 
     def order(j):
         return jnp.where(a < length // 2, (a - 1 - j + 2 * length) % length, (a + 1 + j) % length)
@@ -193,11 +198,45 @@
 
     def to_twin(pos, side):
         k = pos * 2 + side
-        return remote(parts.at[index_of(pos, side, 1 - c)], recv1.at[k], s1.at[k], r1.at[k], twin)
-
-    def load_own(pos, side):
-        k = pos * 2 + side
-        return pltpu.make_async_copy(parts.at[index_of(pos, side, c)], own1.at[k], load.at[k])
+        return remote(parts.at[k * 2], recv1.at[k], s1.at[k], r1.at[k], twin)
+
+    def own_part(pos, side):
+        return parts.at[(pos * 2 + side) * 2 + 1]
+
+    def to_peer(k):
+        return pltpu.make_async_remote_copy(
+            src_ref=embed_sum,
+            dst_ref=embed_in.at[me],
+            send_sem=sx.at[k],
+            recv_sem=rx.at[k],
+            device_id={"proto": (me + k) % n_proto},
+            device_id_type=MESH,
+        )
+
+    def fetches(q, pos, side):
+        slot = q % 2
+        copies = []
+        for w, core in enumerate((1 - c, c)):
+            at = pl.ds(pl.multiple_of(index_of(pos, side, core) * rows, rows), rows)
+            copies += [
+                pltpu.make_async_copy(anchors.at[at, :], a_buf.at[slot, w], load.at[slot, w, 0]),
+                pltpu.make_async_copy(moves.at[at, :], b_buf.at[slot, w], load.at[slot, w, 1]),
+                pltpu.make_async_copy(codes.at[:, at], c_buf.at[slot, w], load.at[slot, w, 2]),
+            ]
+        return copies
+
+    def make(q, pos, side):
+        slot = q % 2
+
+        def one(i, carry):
+            w, at = i // tiles, pl.ds(pl.multiple_of((i % tiles) * tile, tile), tile)
+            anchor, move, code = a_buf[slot, w, at, :], b_buf[slot, w, at, :], c_buf[slot, w, :, at]
+            part, embed = weights(rows_ref[...], tans_ref[...], anchor, move, code, stats_ref)
+            parts[(pos * 2 + side) * 2 + w, at, :] = part
+            embed_sum[...] += embed
+            return carry
+
+        lax.fori_loop(0, 2 * tiles, one, 0)
 
     def to_pair(pos):
         return remote(out2.at[pos], recv2.at[pos], s2.at[pos], r2.at[pos], pair)
@@ -207,15 +246,6 @@
 
     def to_left(pos):
         return remote(out_l.at[pos], recv_r.at[pos], sl.at[pos], rr.at[pos], left)
-
-    for j in range(length):
-        for side in (1 - b, b):
-            load_own(order(j), side).start()
-    greet(a, b, c, length)
-    for side in (1 - b, b):
-        for j in range(length):
-            to_twin(order(j), side).start()
-    embed_in.wait()
 
     def added(dst, srcs):
         def one(i, carry):
@@ -228,23 +258,10 @@
 
         lax.fori_loop(0, rows // step, one, 0)
 
-    for j in range(length):
-        pos = order(j)
-        k = pos * 2 + 1 - b
-        load_own(pos, 1 - b).wait()
-        to_twin(pos, 1 - b).wait_recv()
-        added(out2.at[pos], [own1.at[k], recv1.at[k]])
-        to_pair(pos).start()
-
-    for j in range(length):
-        load_own(order(j), b).wait()
-        to_twin(order(j), b).wait_recv()
-
     def terms(pos):
-        k = pos * 2 + b
-        return [own1.at[k], recv1.at[k], recv2.at[pos]]
-
-    for t in range(length - 1):
+        return [own_part(pos, b), recv1.at[pos * 2 + b], recv2.at[pos]]
+
+    def to_line(t):
         r_pos = length - 1 - (t - a)
         l_pos = t - (length - 1 - a)
 
@@ -278,8 +295,50 @@
 
             to_left(l_pos).start()
 
+    def received(j, crossing):
+        pos = order(j)
+        side = 1 - b if crossing else b
+        to_twin(pos, side).wait_recv()
+        if crossing:
+            added(out2.at[pos], [own_part(pos, side), recv1.at[pos * 2 + side]])
+            to_pair(pos).start()
+
+    turns = [(0, True)]
+    for j in range(1, length):
+        turns += [(j, True), (j - 1, False)]
+    turns += [(length - 1, False)]
+
+    def where(turn):
+        return order(turn[0]), (1 - b if turn[1] else b)
+
+    embed_sum[...] = jnp.zeros_like(embed_sum)
+    for copy in fetches(0, *where(turns[0])):
+        copy.start()
+    greet(a, b, c, length, n_proto)
+    ready = 0
+    for q, turn in enumerate(turns):
+        for copy in fetches(q, *where(turn)):
+            copy.wait()
+        if q + 1 < len(turns):
+            for copy in fetches(q + 1, *where(turns[q + 1])):
+                copy.start()
+        make(q, *where(turn))
+        to_twin(*where(turn)).start()
+        if q + 1 == len(turns):
+            for k in range(1, n_proto):
+                to_peer(k).start()
+        if q > 0:
+            received(*turns[q - 1])
+            if not turns[q - 1][1]:
+                to_line(turns[q - 1][0])
+    received(*turns[-1])
+    embed_in[me] = embed_sum[...]
+    for k in range(1, n_proto):
+        to_peer(k).wait_recv()
+    embeds[index_of(a, b, c)] = functools.reduce(jnp.add, [embed_in[k] for k in range(n_proto)]).astype(BF16)
+
     to_pair(a).wait_recv()
-    final = own1.at[a * 2 + b]
+    final = own_part(a, b)
 
     @pl.when(a > 0)
     def _():
@@ -301,7 +360,7 @@
     def _():
         added(final, terms(a) + [recv_l.at[a], recv_r.at[a]])
 
-    done = pltpu.make_async_copy(final, out.at[index_of(a, b, c)], local.at[1])
+    done = pltpu.make_async_copy(final, out.at[index_of(a, b, c)], local)
     done.start()
     done.wait()
     gather_steps([(embeds, e_send, e_recv), (out, g_send, g_recv)], a, b, c, length)
@@ -319,31 +378,40 @@
         def _():
             to_left(pos).wait_send()
 
-
-def reduce_call(n, parts, embed, collective_id):
+    for k in range(1, n_proto):
+        to_peer(k).wait_send()
+
+
+def reduce_call(n, n_proto, rows_in, tans, stats, anchors, moves, codes, collective_id):
     length = n // 4
-    rows, width = parts.shape[1:]
+    crops, width = rows_in.shape
+    rows = anchors.shape[0] // n
     sems = pltpu.SemaphoreType.DMA
     block = lambda count: pltpu.VMEM((count, rows, width), BF16)
+    near, far = pl.BlockSpec(memory_space=pltpu.VMEM), pl.BlockSpec(memory_space=pl.ANY)
     return pl.pallas_call(
-        functools.partial(reduce_kernel, n),
+        functools.partial(reduce_kernel, n, n_proto),
         out_shape=(
-            jax.ShapeDtypeStruct(parts.shape, BF16),
-            jax.ShapeDtypeStruct((n,) + embed.shape, BF16),
+            jax.ShapeDtypeStruct((n, rows, width), BF16),
+            jax.ShapeDtypeStruct((n, crops, width), BF16),
         ),
-        in_specs=[pl.BlockSpec(memory_space=pl.ANY)] * 2,
-        out_specs=[pl.BlockSpec(memory_space=pl.ANY)] * 2,
+        in_specs=[near, near, near, far, far, far],
+        out_specs=[far, near],
         scratch_shapes=[
-            block(2 * length), block(2 * length), block(length), block(length), block(length),
+            pltpu.VMEM((2, 2, rows, width), BF16), pltpu.VMEM((2, 2, rows, width), BF16),
+            pltpu.VMEM((2, 2, crops, rows), BF16),
+            block(n), block(2 * length), block(length), block(length), block(length),
             block(length), block(length), block(length),
-            sems((2 * length,)), sems((2 * length,)), sems((2 * length,)), sems((length,)), sems((length,)),
-            sems((length,)), sems((length,)), sems((length,)), sems((length,)), sems((2,)),
+            pltpu.VMEM((crops, width), F32), pltpu.VMEM((n_proto, crops, width), F32),
+            sems((2, 2, 3)), sems((2 * length,)), sems((2 * length,)), sems((length,)), sems((length,)),
+            sems((length,)), sems((length,)), sems((length,)), sems((length,)),
+            sems((n_proto,)), sems((n_proto,)), sems,
             sems((4, n)), sems((n,)), sems((4, n)), sems((n,)),
         ],
         compiler_params=pltpu.CompilerParams(
-            collective_id=collective_id, has_side_effects=True, vmem_limit_bytes=48 * MIB
+            collective_id=collective_id, has_side_effects=True, vmem_limit_bytes=58 * MIB
         ),
-    )(parts, embed)
+    )(rows_in, tans, stats, anchors, moves, codes)
 
 
 def dot_t(left, right):
@@ -361,19 +429,24 @@
         weighted[...] = jnp.zeros_like(weighted)
         mass[...] = jnp.zeros_like(mass)
 
-    s = dot_t(rows_ref[...], a_ref[...])
-    pairs = jnp.concatenate([a_ref[...], b_ref[...]], axis=1)
-    tan = dot_t(jnp.concatenate([tans_ref[...], rows_ref[...]], axis=1), pairs)
-    cols = [slice(k, k + LANES) for k in range(0, chunk, LANES)]
-    old = top[...]
-    new = functools.reduce(jnp.maximum, [s[:, k] for k in cols], old)
-    fade = jnp.exp2((old - new) * SCALE)
-    z, w, q = total[...] * fade, weighted[...] * fade, mass[...]
-    for k in cols:
-        e = jnp.exp2((s[:, k] - new) * SCALE)
-        z = z + e
-        w = w + e * tan[:, k]
-        q = q + codes_ref[:, k].astype(F32)
+    left = jnp.concatenate([tans_ref[...], rows_ref[...]], axis=1)
+    new, z, w, q = top[...], total[...], weighted[...], mass[...]
+    part = math.gcd(chunk, 1024)
+    for first in range(0, chunk, part):
+        at = slice(first, first + part)
+        s = dot_t(rows_ref[...], a_ref[at, :])
+        tan = dot_t(left, jnp.concatenate([a_ref[at, :], b_ref[at, :]], axis=1))
+        cols = [slice(k, k + LANES) for k in range(0, part, LANES)]
+        old = new
+        new = functools.reduce(jnp.maximum, [s[:, k] for k in cols], old)
+        fade = jnp.exp2((old - new) * SCALE)
+        z, w = z * fade, w * fade
+        for k in cols:
+            e = jnp.exp2((s[:, k] - new) * SCALE)
+            z = z + e
+            w = w + e * tan[:, k]
+        for k in cols:
+            q = q + codes_ref[:, first + k.start : first + k.stop].astype(F32)
     top[...], total[...], weighted[...], mass[...] = new, z, w, q
 
     @pl.when(i == pl.num_programs(0) - 1)
@@ -396,7 +469,7 @@
 def stats_call(rows, tans, anchors, moves, codes):
     crops, width = rows.shape
     protos = anchors.shape[0]
-    chunk = math.gcd(protos, 1024)
+    chunk = math.gcd(protos, 2048)
     whole = pl.BlockSpec((crops, width), lambda i: (0, 0))
     block = pl.BlockSpec((chunk, width), lambda i: (i, 0))
     return pl.pallas_call(
@@ -406,55 +479,25 @@
         in_specs=[whole, whole, block, block, pl.BlockSpec((crops, chunk), lambda i: (0, i))],
         out_specs=pl.BlockSpec((crops, LANES), lambda i: (0, 0)),
         scratch_shapes=[pltpu.VMEM((crops, LANES), F32)] * 4,
-        compiler_params=pltpu.CompilerParams(vmem_limit_bytes=40 * MIB),
+        compiler_params=pltpu.CompilerParams(vmem_limit_bytes=56 * MIB),
     )(rows, tans, anchors, moves, codes)
 
 
-def weights_kernel(rows_ref, tans_ref, a_ref, b_ref, codes_ref, stats_ref, part_ref, embed_ref):
-    i = pl.program_id(0)
-
-    @pl.when(i == 0)
-    def _():
-        embed_ref[...] = jnp.zeros_like(embed_ref)
-
-    s = dot_t(rows_ref[...], a_ref[...])
-    pairs = jnp.concatenate([a_ref[...], b_ref[...]], axis=1)
-    tan = dot_t(jnp.concatenate([tans_ref[...], rows_ref[...]], axis=1), pairs)
+def weights(rows, tans, anchor, move, code, stats_ref):
+    s = dot_t(rows, anchor)
+    tan = dot_t(jnp.concatenate([tans, rows], axis=1), jnp.concatenate([anchor, move], axis=1))
     peak, gain, mean = stats_ref[:, 0:1], stats_ref[:, 1:2], stats_ref[:, 2:3]
     p = jnp.exp2((s - peak) * SCALE) * gain
     u = (p * (tan - mean)).astype(BF16)
-    v = (TEMP * (p - codes_ref[...].astype(F32))).astype(BF16)
-    embed_ref[...] += jnp.dot(u, a_ref[...], preferred_element_type=F32) + jnp.dot(
-        v, b_ref[...], preferred_element_type=F32
+    v = (TEMP * (p - code.astype(F32))).astype(BF16)
+    embed = jnp.dot(u, anchor, preferred_element_type=F32) + jnp.dot(v, move, preferred_element_type=F32)
+    part = lax.dot_general(
+        jnp.concatenate([u, v], axis=0),
+        jnp.concatenate([rows, tans], axis=0),
+        (((0,), (0,)), ((), ())),
+        preferred_element_type=F32,
     )
-    both = jnp.concatenate([u, v], axis=0)
-    ends = jnp.concatenate([rows_ref[...], tans_ref[...]], axis=0)
-    part_ref[...] = lax.dot_general(
-        both, ends, (((0,), (0,)), ((), ())), preferred_element_type=F32
-    ).astype(BF16)
-
-
-def weights_call(rows, tans, anchors, moves, codes, stats):
-    crops, width = rows.shape
-    protos = anchors.shape[0]
-    chunk = math.gcd(protos, 1024)
-    whole = pl.BlockSpec((crops, width), lambda i: (0, 0))
-    block = pl.BlockSpec((chunk, width), lambda i: (i, 0))
-    return pl.pallas_call(
-        weights_kernel,
-        grid=(protos // chunk,),
-        out_shape=(
-            jax.ShapeDtypeStruct((protos, width), BF16),
-            jax.ShapeDtypeStruct((crops, width), F32),
-        ),
-        in_specs=[
-            whole, whole, block, block,
-            pl.BlockSpec((crops, chunk), lambda i: (0, i)),
-            pl.BlockSpec((crops, LANES), lambda i: (0, 0)),
-        ],
-        out_specs=(block, whole),
-        compiler_params=pltpu.CompilerParams(vmem_limit_bytes=40 * MIB),
-    )(rows, tans, anchors, moves, codes, stats)
+    return part.astype(BF16), embed
 
 
 def body(n, n_proto, features, tangents, anchors, moves, codes, partner):
@@ -472,10 +515,8 @@
     mass = jnp.sum(every[:, 3], axis=0)
     stats = jnp.stack([peak, mass / total, mean], axis=1)
     stats = jnp.pad(stats, ((0, 0), (0, LANES - 3)))
-    parts, embed = weights_call(rows, tans, anchors, moves, codes, stats)
-    embed = lax.psum(embed, "proto").astype(BF16)
     protos = anchors.shape[0]
-    out, embeds = reduce_call(n, parts.reshape(n, protos // n, width), embed, 2)
+    out, embeds = reduce_call(n, n_proto, rows, tans, stats, anchors, moves, codes, 2)
     hvp_embed = jnp.take(embeds.reshape(n * crops, width), partner, axis=0)
     return hvp_embed, out.reshape(protos, width)
 

time: 241 us -> 189 us (0.78)
  Pallas kernels: 204 us -> 164 us
  blocking collectives: 15.2 us -> 5.01 us
    pallas_call x2 -> x1, Pallas kernels: 152 us -> 116 us  [reduce_call(): pl.pallas_call(functools.partial(reduce_kernel, n, n_proto), out_shape=(j...]
    psum x1 -> x0, blocking collectives: 10.2 us -> none  [body(): embed = lax.psum(embed, 'proto').astype(BF16)]
    unnamed x5 -> x1, local copies, waits for them, and re-layouts: 13.9 us -> 7.1 us
    pallas_call x1, Pallas kernels: 29.2 us -> 23.5 us  [stats_call(): pl.pallas_call(stats_kernel, grid=(protos // chunk,), out_shape=jax.Shape...]
where the time goes in v2:
time: 189 us; the launch traced here: 188 us
  Pallas kernels  164 us (87%)
  local copies, waits for them, and re-layouts  14.5 us (8%)
  blocking collectives  5.01 us (3%)
  other arithmetic  3.9 us (2%)
    pallas_call x1, Pallas kernels, reduce_call(): pl.pallas_call(functools.partial(reduce_kernel, n, n_proto), out_shape=(j...  116 us
    pallas_call x1, Pallas kernels, gather_call(): pl.pallas_call(functools.partial(gather_kernel, n), out_shape=jax.ShapeDt...  25 us
    pallas_call x1, Pallas kernels, stats_call(): pl.pallas_call(stats_kernel, grid=(protos // chunk,), out_shape=jax.Shape...  23.5 us
    unnamed x1, local copies, waits for them, and re-layouts  7.1 us
    psum x1, blocking collectives, body(): every = lax.psum(jnp.where(mine[:, None, None], local[None], 0.0), 'proto')  5.01 us

profile of v2, /device:TPU:0, one launch (start us, length us, event | category | flops | bytes accessed | tf_op | source)
XLA Modules:
  0.0 188.3 jit_solution(16308234675945393243)
XLA Ops:
  0.6 0.7 compare_and_fusion
  1.3 0.7 compare_select_fusion
  2.0 1.5 pad_maximum_fusion.x
  3.6 25.0 %shard_map.77 = bf16[16,256,256]{2,1,0:T(8,128)(2,1)} custom-call(bf16[256,256]{1,0:T(8,128)(2,1)} %pad_maximum_fusion.x), custom_call_target="tpu_custom_call" | custom-call | tf_op jit(solution)/shard_map/pallas_call | solution.py:163
  28.5 2.8 %gather_fusion = bf16[256,256]{1,0:T(8,128)(2,1)S(1)} fusion(bf16[4096,256]{1,0:T(8,128)(2,1)} %bitcast.31, s32[1024]{0:T(1024)S(1)} %pad_clamp_fusion), kind=kCustom, calls=%fused_computation | custom fusion | bytes 263168 | tf_op jit(solution)/shard_map/jit(_take)/gather | solution.py:506
  31.4 0.1 broadcast_select_fusion
  31.5 0.6 fusion.6
  32.1 23.5 %shard_map.78 = f32[256,128]{1,0:T(8,128)} custom-call(bf16[256,128]{1,0:T(8,128)(2,1)} %get-tuple-element.11.rows_ref, bf16[256,128]{1,0:T(8,128)(2,1)} %get-tuple-element.10.tans_ref, bf16[32768,128]{1,0:T(8,128)(2,1)} %anchors.1, bf16[32768,128]{1,0:T(8,128)(2,1)} %moves.1, bf16[256,32768]{1,0:T(8,128)(2,1)} %codes.1), custom_call_target="tpu_custom_call" | custom-call | tf_op jit(solution)/shard_map/pallas_call | solution.py:475
  55.6 0.9 slice_bitcast_fusion
  56.5 0.1 copy.21
  56.6 0.1 broadcast_select_fusion.2
  56.7 5.0 %psum.7 = f32[2,4,256]{2,0,1:T(2,128)S(1)} all-reduce(f32[2,4,256]{2,0,1:T(2,128)S(1)} %broadcast_select_fusion.2), channel_id=1, replica_groups=mesh['dp'=16,'proto'=2] {'proto'}, use_global_device_ids=true, to_apply=%region_0.1 | all-reduce | flops 2048 | bytes 16384 | tf_op jit(solution)/shard_map/psum | solution.py:510
  61.7 0.1 copy.22
  61.9 0.7 pad.4.stats_ref
  62.6 115.8 %shard_map.79 = (bf16[16,2048,128]{2,1,0:T(8,128)(2,1)}, bf16[16,256,128]{2,1,0:T(8,128)(2,1)}) custom-call(bf16[256,128]{1,0:T(8,128)(2,1)} %get-tuple-element.11.rows_ref, bf16[256,128]{1,0:T(8,128)(2,1)} %get-tuple-element.10.tans_ref, f32[256,128]{1,0:T(8,128)} %pad.4.stats_ref, bf16[32768,128]{1,0:T(8,128)(2,1)} %anchors.1, bf16[32768,128]{1,0:T(8,128)(2,1)} %moves.1, ...), custom_call_target="tpu_custom_call" | custom-call | tf_op jit(solution)/shard_map/pallas_call | solution.py:392
  178.4 2.1 %gather_fusion.1 = bf16[256,128]{1,0:T(8,128)(2,1)S(1)} fusion(bf16[4096,128]{1,0:T(8,128)(2,1)} %bitcast.32, s32[1024]{0:T(1024)S(1)} %pad_clamp_fusion), kind=kCustom, calls=%fused_computation.1 | custom fusion | bytes 132096 | tf_op jit(solution)/shard_map/jit(_take)/gather | solution.py:520
  180.5 0.7 broadcast_select_fusion.1
  181.2 7.1 %copy.24 = bf16[32768,128]{1,0:T(8,128)(2,1)} copy(bf16[32768,128]{1,0:T(8,128)(2,1)} %bitcast.30) | data formatting | bytes 16777216
  (6 shorter events, 0.1 us)

commit v3 on v2

--- a/solution.py
+++ b/solution.py
@@ -55,14 +55,14 @@
     def __init__(self, arrays, block, kind, target):
         self.copies = [
             pltpu.make_async_remote_copy(
-                src_ref=out.at[block],
-                dst_ref=out.at[block],
+                src_ref=out.at[block, at],
+                dst_ref=out.at[block, at],
                 send_sem=send.at[kind, block],
                 recv_sem=recv.at[block],
                 device_id={"dp": target},
                 device_id_type=MESH,
             )
-            for out, send, recv in arrays
+            for out, send, recv, at in arrays
         ]
 
     def start(self):
@@ -78,10 +78,13 @@
             copy.wait_recv()
 
 
-def gather_steps(arrays, a, b, c, length):
+def gather_steps(arrays, early, a, b, c, length):
     def copy(block, kind, target):
         return Copies(arrays, block, kind, target)
 
+    def soon(block, kind, target):
+        return Copies(early, block, kind, target)
+
     right, left = index_of(a + 1, b, c), index_of(a - 1, b, c)
     pair, twin = index_of(a, 1 - b, c), index_of(a, b, 1 - c)
 
@@ -103,24 +106,52 @@
 
         copy(block, 2, pair).start()
         copy(block, 3, twin).start()
+
+    def spread_soon(block, to_right, to_left):
+        if to_right:
+
+            @pl.when(a < length - 1)
+            def _():
+                soon(block, 0, right).start()
+
+        if to_left:
+
+            @pl.when(a > 0)
+            def _():
+                soon(block, 1, left).start()
+
+        soon(block, 3, twin).start()
 
     def from_pair(pos):
         block = index_of(pos, 1 - b, c)
         copy(block, 2, pair).wait_recv()
         copy(block, 3, twin).start()
 
+    if early:
+        soon(line_block(a), 2, pair).start()
     spread(line_block(a), True, True)
+    if early:
+        spread_soon(line_block(a), True, True)
+        other = index_of(a, 1 - b, c)
+        soon(other, 2, pair).wait_recv()
+        spread_soon(other, True, True)
     for k in range(1, length):
 
         @pl.when(a - k >= 0)
         def _():
             copy(line_block(a - k), 0, right).wait_recv()
             spread(line_block(a - k), True, False)
+            for side in (b, 1 - b) if early else ():
+                soon(index_of(a - k, side, c), 0, right).wait_recv()
+                spread_soon(index_of(a - k, side, c), True, False)
 
         @pl.when(a + k < length)
         def _():
             copy(line_block(a + k), 1, left).wait_recv()
             spread(line_block(a + k), False, True)
+            for side in (b, 1 - b) if early else ():
+                soon(index_of(a + k, side, c), 1, left).wait_recv()
+                spread_soon(index_of(a + k, side, c), False, True)
 
     from_pair(a)
     for k in range(1, length):
@@ -136,49 +167,69 @@
     for pos in range(length):
         for side in range(2):
             copy(index_of(pos, side, 1 - c), 3, twin).wait_recv()
+            if early:
+                soon(index_of(pos, side, 1 - c), 3, twin).wait_recv()
+    if early:
+        soon(line_block(a), 2, pair).wait_send()
     for pos in range(length):
         copy(line_block(pos), 2, pair).wait_send()
         for side in range(2):
             copy(index_of(pos, side, c), 3, twin).wait_send()
+            if early:
+                soon(index_of(pos, side, c), 3, twin).wait_send()
 
         @pl.when(jnp.logical_and(a < length - 1, pos <= a))
         def _():
             copy(line_block(pos), 0, right).wait_send()
+            for side in range(2) if early else ():
+                soon(index_of(pos, side, c), 0, right).wait_send()
 
         @pl.when(jnp.logical_and(a > 0, pos >= a))
         def _():
             copy(line_block(pos), 1, left).wait_send()
-
-
-def gather_kernel(n, x, out, send, recv, local):
+            for side in range(2) if early else ():
+                soon(index_of(pos, side, c), 1, left).wait_send()
+
+
+def gather_kernel(n, x, y, out, send, recv, local):
     a, b, c, length = place(n)
-    own = pltpu.make_async_copy(x, out.at[index_of(a, b, c)], local)
-    own.start()
+    rows, width = x.shape
+    mine = index_of(a, b, c)
+    own = [
+        pltpu.make_async_copy(part, out.at[mine, :, pl.ds(k * width, width)], local.at[k])
+        for k, part in enumerate((x, y))
+    ]
+    for copy in own:
+        copy.start()
     greet(a, b, c, length)
-    own.wait()
-    gather_steps([(out, send, recv)], a, b, c, length)
-
-
-def gather_call(n, x, collective_id):
+    for copy in own:
+        copy.wait()
+    gather_steps([(out, send, recv, pl.ds(0, rows))], [], a, b, c, length)
+
+
+def gather_call(n, x, y, collective_id):
+    rows, width = x.shape
+    near = pl.BlockSpec(memory_space=pltpu.VMEM)
     return pl.pallas_call(
         functools.partial(gather_kernel, n),
-        out_shape=jax.ShapeDtypeStruct((n,) + x.shape, x.dtype),
-        in_specs=[pl.BlockSpec(memory_space=pltpu.VMEM)],
-        out_specs=pl.BlockSpec(memory_space=pltpu.VMEM),
+        out_shape=jax.ShapeDtypeStruct((n, rows, 2 * width), x.dtype),
+        in_specs=[near, near],
+        out_specs=near,
         scratch_shapes=[
             pltpu.SemaphoreType.DMA((4, n)),
             pltpu.SemaphoreType.DMA((n,)),
-            pltpu.SemaphoreType.DMA,
+            pltpu.SemaphoreType.DMA((2,)),
         ],
         compiler_params=pltpu.CompilerParams(
             collective_id=collective_id, has_side_effects=True, vmem_limit_bytes=56 * MIB
         ),
-    )(x)
+    )(x, y)
 
 
 def reduce_kernel(n, n_proto, rows_ref, tans_ref, stats_ref, anchors, moves, codes, out, embeds,
                   a_buf, b_buf, c_buf, parts, recv1, recv2, recv_l, recv_r, out2, out_l, out_r, embed_sum, embed_in,
-                  load, s1, r1, s2, r2, sl, sr, rl, rr, sx, rx, local, g_send, g_recv, e_send, e_recv):
+                  load, s1, r1, s2, r2, sl, sr, rl, rr, sx, rx, local, g_send, g_recv, h_send, h_recv, e_send, e_recv,
+                  stats, stats_in, st, rt):
     a, b, c, length = place(n)
     me = lax.axis_index("proto")
     rows = parts.shape[1]
@@ -212,6 +263,26 @@
             device_id={"proto": (me + k) % n_proto},
             device_id_type=MESH,
         )
+
+    def stats_to(k):
+        return pltpu.make_async_remote_copy(
+            src_ref=stats_ref,
+            dst_ref=stats_in.at[me],
+            send_sem=st.at[k],
+            recv_sem=rt.at[k],
+            device_id={"proto": (me + k) % n_proto},
+            device_id_type=MESH,
+        )
+
+    def join_stats():
+        every = [stats_in[k] for k in range(n_proto)]
+        peak = functools.reduce(jnp.maximum, [x[:, 0:1] for x in every])
+        scale = [jnp.exp2((x[:, 0:1] - peak) * SCALE) for x in every]
+        total = functools.reduce(jnp.add, [x[:, 1:2] * f for x, f in zip(every, scale)])
+        tangent = functools.reduce(jnp.add, [x[:, 2:3] * f for x, f in zip(every, scale)])
+        mass = functools.reduce(jnp.add, [x[:, 3:4] for x in every])
+        lane = lax.broadcasted_iota(jnp.int32, stats.shape, 1)
+        stats[...] = jnp.where(lane == 0, peak, jnp.where(lane == 1, mass / total, tangent / total))
 
     def fetches(q, pos, side):
         slot = q % 2
@@ -231,7 +302,7 @@
         def one(i, carry):
             w, at = i // tiles, pl.ds(pl.multiple_of((i % tiles) * tile, tile), tile)
             anchor, move, code = a_buf[slot, w, at, :], b_buf[slot, w, at, :], c_buf[slot, w, :, at]
-            part, embed = weights(rows_ref[...], tans_ref[...], anchor, move, code, stats_ref)
+            part, embed = weights(rows_ref[...], tans_ref[...], anchor, move, code, stats)
             parts[(pos * 2 + side) * 2 + w, at, :] = part
             embed_sum[...] += embed
             return carry
@@ -315,7 +386,12 @@
     for copy in fetches(0, *where(turns[0])):
         copy.start()
     greet(a, b, c, length, n_proto)
-    ready = 0
+    for k in range(1, n_proto):
+        stats_to(k).start()
+    stats_in[me] = stats_ref[...]
+    for k in range(1, n_proto):
+        stats_to(k).wait_recv()
+    join_stats()
     for q, turn in enumerate(turns):
         for copy in fetches(q, *where(turn)):
             copy.wait()
@@ -363,7 +439,10 @@
     done = pltpu.make_async_copy(final, out.at[index_of(a, b, c)], local)
     done.start()
     done.wait()
-    gather_steps([(embeds, e_send, e_recv), (out, g_send, g_recv)], a, b, c, length)
+    crops = embeds.shape[1]
+    cut = rows // 8
+    whole = [(embeds, e_send, e_recv, pl.ds(0, crops)), (out, g_send, g_recv, pl.ds(cut, rows - cut))]
+    gather_steps(whole, [(out, h_send, h_recv, pl.ds(0, cut))], a, b, c, length)
 
     for pos in range(length):
         for side in range(2):
@@ -380,6 +459,7 @@
 
     for k in range(1, n_proto):
         to_peer(k).wait_send()
+        stats_to(k).wait_send()
 
 
 def reduce_call(n, n_proto, rows_in, tans, stats, anchors, moves, codes, collective_id):
@@ -406,7 +486,9 @@
             sems((2, 2, 3)), sems((2 * length,)), sems((2 * length,)), sems((length,)), sems((length,)),
             sems((length,)), sems((length,)), sems((length,)), sems((length,)),
             sems((n_proto,)), sems((n_proto,)), sems,
-            sems((4, n)), sems((n,)), sems((4, n)), sems((n,)),
+            sems((4, n)), sems((n,)), sems((4, n)), sems((n,)), sems((4, n)), sems((n,)),
+            pltpu.VMEM((crops, LANES), F32), pltpu.VMEM((n_proto, crops, LANES), F32),
+            sems((n_proto,)), sems((n_proto,)),
         ],
         compiler_params=pltpu.CompilerParams(
             collective_id=collective_id, has_side_effects=True, vmem_limit_bytes=58 * MIB
@@ -418,6 +500,14 @@
     return lax.dot_general(left, right, (((1,), (1,)), ((), ())), preferred_element_type=F32)
 
 
+def products(rows, tans, anchor, move):
+    crops = rows.shape[0]
+    upper = jnp.concatenate([rows, jnp.zeros_like(rows)], axis=1)
+    lower = jnp.concatenate([tans, rows], axis=1)
+    both = dot_t(jnp.concatenate([upper, lower], axis=0), jnp.concatenate([anchor, move], axis=1))
+    return both[:crops], both[crops:]
+
+
 def stats_kernel(rows_ref, tans_ref, a_ref, b_ref, codes_ref, out_ref, top, total, weighted, mass):
     i = pl.program_id(0)
     chunk = a_ref.shape[0]
@@ -429,13 +519,11 @@
         weighted[...] = jnp.zeros_like(weighted)
         mass[...] = jnp.zeros_like(mass)
 
-    left = jnp.concatenate([tans_ref[...], rows_ref[...]], axis=1)
     new, z, w, q = top[...], total[...], weighted[...], mass[...]
     part = math.gcd(chunk, 1024)
     for first in range(0, chunk, part):
         at = slice(first, first + part)
-        s = dot_t(rows_ref[...], a_ref[at, :])
-        tan = dot_t(left, jnp.concatenate([a_ref[at, :], b_ref[at, :]], axis=1))
+        s, tan = products(rows_ref[...], tans_ref[...], a_ref[at, :], b_ref[at, :])
         cols = [slice(k, k + LANES) for k in range(0, part, LANES)]
         old = new
         new = functools.reduce(jnp.maximum, [s[:, k] for k in cols], old)
@@ -484,8 +572,7 @@
 
 
 def weights(rows, tans, anchor, move, code, stats_ref):
-    s = dot_t(rows, anchor)
-    tan = dot_t(jnp.concatenate([tans, rows], axis=1), jnp.concatenate([anchor, move], axis=1))
+    s, tan = products(rows, tans, anchor, move)
     peak, gain, mean = stats_ref[:, 0:1], stats_ref[:, 1:2], stats_ref[:, 2:3]
     p = jnp.exp2((s - peak) * SCALE) * gain
     u = (p * (tan - mean)).astype(BF16)
@@ -502,22 +589,13 @@
 
 def body(n, n_proto, features, tangents, anchors, moves, codes, partner):
     crops, width = features.shape
-    gathered = gather_call(n, jnp.concatenate([features, tangents], axis=1), 1)
-    swapped = jnp.take(gathered.reshape(n * crops, 2 * width), partner, axis=0)
+    protos = anchors.shape[0]
+    gathered = gather_call(n, features, tangents, 1)
+    swapped = gathered.reshape(n * crops, 2 * width).at[partner].get(mode="promise_in_bounds")
     rows, tans = swapped[:, :width], swapped[:, width:]
-    local = stats_call(rows, tans, anchors, moves, codes)[:, :4].T
-    mine = jnp.arange(n_proto) == lax.axis_index("proto")
-    every = lax.psum(jnp.where(mine[:, None, None], local[None], 0.0), "proto")
-    peak = jnp.max(every[:, 0], axis=0)
-    scale = jnp.exp2((every[:, 0] - peak) * SCALE)
-    total = jnp.sum(every[:, 1] * scale, axis=0)
-    mean = jnp.sum(every[:, 2] * scale, axis=0) / total
-    mass = jnp.sum(every[:, 3], axis=0)
-    stats = jnp.stack([peak, mass / total, mean], axis=1)
-    stats = jnp.pad(stats, ((0, 0), (0, LANES - 3)))
-    protos = anchors.shape[0]
-    out, embeds = reduce_call(n, n_proto, rows, tans, stats, anchors, moves, codes, 2)
-    hvp_embed = jnp.take(embeds.reshape(n * crops, width), partner, axis=0)
+    local = stats_call(rows, tans, anchors, moves, codes)
+    out, embeds = reduce_call(n, n_proto, rows, tans, local, anchors, moves, codes, 2)
+    hvp_embed = embeds.reshape(n * crops, width).at[partner].get(mode="promise_in_bounds")
     return hvp_embed, out.reshape(protos, width)
 
 

time: 189 us -> 186 us (0.984)
  Pallas kernels: 164 us -> 170 us
  blocking collectives: 5.01 us -> 0 us
  other arithmetic: 3.9 us -> 0.69 us
    pallas_call x1, Pallas kernels: 116 us -> 122 us  [reduce_call(): pl.pallas_call(functools.partial(reduce_kernel, n, n_proto), out_shape=(j...]
    psum x1 -> x0, blocking collectives: 5.01 us -> none  [body(): every = lax.psum(jnp.where(mine[:, None, None], local[None], 0.0), 'proto')]
where the time goes in v3:
time: 186 us; the launch traced here: 185 us
  Pallas kernels  170 us (91%)
  local copies, waits for them, and re-layouts  13.3 us (7%)
    pallas_call x1, Pallas kernels, reduce_call(): pl.pallas_call(functools.partial(reduce_kernel, n, n_proto), out_shape=(j...  122 us
    pallas_call x1, Pallas kernels, gather_call(): pl.pallas_call(functools.partial(gather_kernel, n), out_shape=jax.ShapeDt...  24.8 us
    pallas_call x1, Pallas kernels, stats_call(): pl.pallas_call(stats_kernel, grid=(protos // chunk,), out_shape=jax.Shape...  23.9 us
    unnamed x1, local copies, waits for them, and re-layouts  7.1 us

profile of v3, /device:TPU:0, one launch (start us, length us, event | category | flops | bytes accessed | tf_op | source)
XLA Modules:
  0.0 184.9 jit_solution(8116092549791532943)
XLA Ops:
  0.6 0.7 compare_select_fusion
  1.3 24.8 %shard_map.77 = bf16[16,256,256]{2,1,0:T(8,128)(2,1)} custom-call(bf16[256,128]{1,0:T(8,128)(2,1)} %x.1, bf16[256,128]{1,0:T(8,128)(2,1)} %y.1), custom_call_target="tpu_custom_call" | custom-call | tf_op jit(solution)/shard_map/pallas_call | solution.py:213
  26.2 2.8 %gather_fusion = bf16[256,256]{1,0:T(8,128)(2,1)S(1)} fusion(bf16[4096,256]{1,0:T(8,128)(2,1)} %bitcast.4, s32[1024]{0:T(1024)S(1)} %pad_clamp_fusion), kind=kCustom, calls=%fused_computation | custom fusion | bytes 263168 | tf_op jit(solution)/shard_map/gather | solution.py:594
  29.0 0.6 fusion
  29.6 23.9 %shard_map.78.stats_ref = f32[256,128]{1,0:T(8,128)} custom-call(bf16[256,128]{1,0:T(8,128)(2,1)} %get-tuple-element.7.rows_ref, bf16[256,128]{1,0:T(8,128)(2,1)} %get-tuple-element.6.tans_ref, bf16[32768,128]{1,0:T(8,128)(2,1)} %anchors.1, bf16[32768,128]{1,0:T(8,128)(2,1)} %moves.1, bf16[256,32768]{1,0:T(8,128)(2,1)} %codes.1), custom_call_target="tpu_custom_call" | custom-call | tf_op jit(solution)/shard_map/pallas_call | solution.py:563
  53.5 121.6 %shard_map.79 = (bf16[16,2048,128]{2,1,0:T(8,128)(2,1)}, bf16[16,256,128]{2,1,0:T(8,128)(2,1)}) custom-call(bf16[256,128]{1,0:T(8,128)(2,1)} %get-tuple-element.7.rows_ref, bf16[256,128]{1,0:T(8,128)(2,1)} %get-tuple-element.6.tans_ref, f32[256,128]{1,0:T(8,128)} %shard_map.78.stats_ref, bf16[32768,128]{1,0:T(8,128)(2,1)} %anchors.1, ...), custom_call_target="tpu_custom_call" | custom-call | tf_op jit(solution)/shard_map/pallas_call | solution.py:472
  175.1 2.7 %gather_fusion.1 = bf16[256,128]{1,0:T(8,128)(2,1)} fusion(bf16[4096,128]{1,0:T(8,128)(2,1)} %bitcast.5, s32[1024]{0:T(1024)S(1)} %pad_clamp_fusion), kind=kCustom, calls=%fused_computation.1 | custom fusion | bytes 132096 | tf_op jit(solution)/shard_map/gather | solution.py:598
  177.8 7.1 %copy.9 = bf16[32768,128]{1,0:T(8,128)(2,1)} copy(bf16[32768,128]{1,0:T(8,128)(2,1)} %bitcast.3) | data formatting | bytes 16777216
  (1 shorter events, 0.0 us)

commit v4 on v3

--- a/solution.py
+++ b/solution.py
@@ -557,7 +557,7 @@
 def stats_call(rows, tans, anchors, moves, codes):
     crops, width = rows.shape
     protos = anchors.shape[0]
-    chunk = math.gcd(protos, 2048)
+    chunk = math.gcd(protos, 4096)
     whole = pl.BlockSpec((crops, width), lambda i: (0, 0))
     block = pl.BlockSpec((chunk, width), lambda i: (i, 0))
     return pl.pallas_call(

time: 186 us -> 182 us (0.978)
  Pallas kernels: 170 us -> 167 us
    pallas_call x1, Pallas kernels: 23.9 us -> 20.3 us  [stats_call(): pl.pallas_call(stats_kernel, grid=(protos // chunk,), out_shape=jax.Shape...]
where the time goes in v4:
time: 182 us; the launch traced here: 181 us
  Pallas kernels  167 us (92%)
  local copies, waits for them, and re-layouts  13.3 us (7%)
    pallas_call x1, Pallas kernels, reduce_call(): pl.pallas_call(functools.partial(reduce_kernel, n, n_proto), out_shape=(j...  121 us
    pallas_call x1, Pallas kernels, gather_call(): pl.pallas_call(functools.partial(gather_kernel, n), out_shape=jax.ShapeDt...  24.8 us
    pallas_call x1, Pallas kernels, stats_call(): pl.pallas_call(stats_kernel, grid=(protos // chunk,), out_shape=jax.Shape...  20.3 us
    unnamed x1, local copies, waits for them, and re-layouts  7.1 us

profile of v4, /device:TPU:0, one launch (start us, length us, event | category | flops | bytes accessed | tf_op | source)
XLA Modules:
  0.0 181.2 jit_solution(9062161793216767970)
XLA Ops:
  0.6 0.7 compare_select_fusion
  1.3 24.8 %shard_map.77 = bf16[16,256,256]{2,1,0:T(8,128)(2,1)} custom-call(bf16[256,128]{1,0:T(8,128)(2,1)} %x.1, bf16[256,128]{1,0:T(8,128)(2,1)} %y.1), custom_call_target="tpu_custom_call" | custom-call | tf_op jit(solution)/shard_map/pallas_call | solution.py:213
  26.2 2.8 %gather_fusion = bf16[256,256]{1,0:T(8,128)(2,1)S(1)} fusion(bf16[4096,256]{1,0:T(8,128)(2,1)} %bitcast.4, s32[1024]{0:T(1024)S(1)} %pad_clamp_fusion), kind=kCustom, calls=%fused_computation | custom fusion | bytes 263168 | tf_op jit(solution)/shard_map/gather | solution.py:594
  29.0 0.6 fusion
  29.6 20.3 %shard_map.78.stats_ref = f32[256,128]{1,0:T(8,128)} custom-call(bf16[256,128]{1,0:T(8,128)(2,1)} %get-tuple-element.7.rows_ref, bf16[256,128]{1,0:T(8,128)(2,1)} %get-tuple-element.6.tans_ref, bf16[32768,128]{1,0:T(8,128)(2,1)} %anchors.1, bf16[32768,128]{1,0:T(8,128)(2,1)} %moves.1, bf16[256,32768]{1,0:T(8,128)(2,1)} %codes.1), custom_call_target="tpu_custom_call" | custom-call | tf_op jit(solution)/shard_map/pallas_call | solution.py:563
  49.9 121.5 %shard_map.79 = (bf16[16,2048,128]{2,1,0:T(8,128)(2,1)}, bf16[16,256,128]{2,1,0:T(8,128)(2,1)}) custom-call(bf16[256,128]{1,0:T(8,128)(2,1)} %get-tuple-element.7.rows_ref, bf16[256,128]{1,0:T(8,128)(2,1)} %get-tuple-element.6.tans_ref, f32[256,128]{1,0:T(8,128)} %shard_map.78.stats_ref, bf16[32768,128]{1,0:T(8,128)(2,1)} %anchors.1, ...), custom_call_target="tpu_custom_call" | custom-call | tf_op jit(solution)/shard_map/pallas_call | solution.py:472
  171.4 2.7 %gather_fusion.1 = bf16[256,128]{1,0:T(8,128)(2,1)} fusion(bf16[4096,128]{1,0:T(8,128)(2,1)} %bitcast.5, s32[1024]{0:T(1024)S(1)} %pad_clamp_fusion), kind=kCustom, calls=%fused_computation.1 | custom fusion | bytes 132096 | tf_op jit(solution)/shard_map/gather | solution.py:598
  174.1 7.1 %copy.9 = bf16[32768,128]{1,0:T(8,128)(2,1)} copy(bf16[32768,128]{1,0:T(8,128)(2,1)} %bitcast.3) | data formatting | bytes 16777216
  (1 shorter events, 0.0 us)
